TPU v7x, 32 devices: a whole 2x2x4 slice. The times are simulated.
32 devices in a mesh: groups: 2 (over x), lon: 16 (over z, y, core).
Axes of the slice: x: 2, y: 2, z: 4, core: 2. Of those that a mesh axis runs over, the one named last changes fastest.
Arguments:
- latlon_fields: bfloat16 [32, 32, 2048], P('groups', 'lon'), parts along dimension 0, may hold values from -6 to 6
- remap_table: int32 [2, 32, 2048], P(None, None, 'lon'), may hold values from 0 to 2047, as said below
- kernel_first: bfloat16 [3, 3, 64, 16], replicated, may hold values from -0.5 to 0.5
- kernel_second: bfloat16 [3, 3, 64, 64], replicated, may hold values from -0.25 to 0.25
- kernel_down: bfloat16 [3, 3, 128, 64], replicated, may hold values from -0.25 to 0.25
- kernel_coarse: bfloat16 [3, 3, 128, 128], replicated, may hold values from -0.1875 to 0.1875
- kernel_up: bfloat16 [3, 3, 64, 128], replicated, may hold values from -0.375 to 0.375
- kernel_merge: bfloat16 [3, 3, 64, 128], replicated, may hold values from -0.1875 to 0.1875
- projection: bfloat16 [8, 64], replicated, may hold values from -0.75 to 0.75
Outputs:
- forecast: float32 [16, 32, 2048], P('groups', None, 'lon'), parts along dimension 0
There are 2 independent parts, one for each index of `groups`. A program takes and returns all parts, laid end to end along the dimension named above; an argument that names none is the same for every part. Nothing has to cross between parts.
Inputs may be any that keep to these rules, and one draw needn't show every extreme that they name: remap_table[0] is a lat-lon row below 32; remap_table[1] is a lat-lon column, and for a grid cell in column w it lies in the same block of 128 columns as w, that is between (w // 128) * 128 and (w // 128) * 128 + 127.
All inputs are finite; a program needn't handle non-finite values.
Results may differ from a plain program's by a relative error of at most 0.00084.
Values may be sent and summed in bfloat16 or wider, within the bound.
A program may use at most 128 MiB of HBM per device.

v0:
```python
import functools

import jax
import jax.numpy as jnp
from jax import lax
from jax.experimental import pallas as pl
from jax.experimental.pallas import tpu as pltpu
from jax.sharding import PartitionSpec as P

MESH = pl.DeviceIdType.MESH
F32 = jnp.float32
BF16 = jnp.bfloat16
HALO = 8
PER = 8
OFFSETS = (0, 1, 2, -1)
NT = (((1,), (1,)), ((), ()))


def dot_nt(a, b):
    return lax.dot_general(a, b, NT, preferred_element_type=F32)


def silu(x):
    half = 0.5 * x
    return half * jnp.tanh(half) + half


def clear(*arrays):
    for w in arrays:
        w[...] = jnp.zeros_like(w)


def fill(w, kernel, cin, first_in):
    C = kernel.shape[2]
    for q in range(2):
        for p in range(2):
            for a in range(4):
                for l, off in enumerate(OFFSETS):
                    kr, kcol = a - q, off - p + 1
                    if 0 <= kr < 3 and 0 <= kcol < 3:
                        at = (q * 2 + p) * C
                        lane = a * 4 * cin + l * cin
                        w[at : at + C, lane : lane + cin] = kernel[kr, kcol][:, first_in : first_in + cin]


def fine_weights(k1, k2, km, w1, wlast, wfirst, wnext, w2, wma, wmb):
    C, channels = k1.shape[2], k1.shape[3]
    wide = PER * channels
    clear(w1, wlast, wfirst, wnext, w2, wma, wmb)
    for p in range(2):
        for l, off in enumerate(OFFSETS):
            if not 0 <= off - p + 1 < 3:
                continue
            k = [k1[kr, off - p + 1] for kr in range(3)]
            lane = l * wide
            for r in range(PER):
                at = (r * 2 + p) * C
                for kr in range(3):
                    if 0 <= r + kr - 1 < PER:
                        to = lane + (r + kr - 1) * channels
                        w1[at : at + C, to : to + channels] = k[kr]
            end = lane + (PER - 1) * channels
            wlast[p * C : (p + 1) * C, end : end + channels] = k[0]
            wfirst[p * C : (p + 1) * C, lane : lane + channels] = k[0]
            wnext[p * C : (p + 1) * C, lane : lane + channels] = k[2]
    fill(w2, k2, C, 0)
    fill(wma, km, C, 0)
    fill(wmb, km, C, C)


def coarse_weights(kd, kc, ku, kp, wd, wc, wu, wp):
    C2, C = kd.shape[2], kd.shape[3]
    COUT = kp.shape[0]
    clear(wd, wc, wu, wp)
    for a in range(3):
        for l, kcol in ((0, 1), (1, 2), (3, 0)):
            wd[:, a * 4 * C + l * C : a * 4 * C + (l + 1) * C] = kd[a, kcol]
        for s, kcol in enumerate((1, 2, 0)):
            wc[:, (a * 3 + s) * C2 : (a * 3 + s + 1) * C2] = kc[a, kcol]
    for q, rows in ((0, ((0, 1),)), (1, ((0, 0), (1, 2)))):
        for p, columns in ((0, ((0, 1),)), (1, ((0, 0), (1, 2)))):
            at = (q * 2 + p) * C
            for ri, kr in rows:
                for ci, kcol in columns:
                    lane = (ri * 2 + ci) * C2
                    wu[at : at + C, lane : lane + C2] = ku[kr, kcol]
    for g in range(4):
        wp[g * COUT : (g + 1) * COUT, g * C : (g + 1) * C] = kp[...].astype(F32)


def exchange_kernel(n, lat_ref, tab_ref, k1, k2, kd, kc, ku, km, kp,
                    own_ref, left_ref, right_ref, anti_ref, anti_left_ref, anti_right_ref,
                    w1, wlast, wfirst, wnext, w2, wd, wc, wu, wma, wmb, wp,
                    recv, edge, send_sem, recv_sem, own_sem, hsend, hrecv):
    me = lax.axis_index("lon")
    group = lax.axis_index("groups")
    cols = recv.shape[2]
    height = tab_ref.shape[1]
    per = height // own_ref.shape[0]
    channels = own_ref.shape[2] // per
    barrier = pltpu.get_barrier_semaphore()

    def greet(d, carry):
        pl.semaphore_signal(barrier, inc=1, device_id=(group, lax.rem(me + d, n)), device_id_type=MESH)
        return carry

    lax.fori_loop(1, n, greet, 0)
    mine = pltpu.make_async_copy(lat_ref.at[:, pl.ds(pl.multiple_of(me * cols, cols), cols)], recv.at[me], own_sem)
    mine.start()
    coarse_weights(kd, kc, ku, kp, wd, wc, wu, wp)
    pl.semaphore_wait(barrier, n - 1)

    def block_copy(d, slot):
        target = lax.rem(me + d, n)
        return pltpu.make_async_remote_copy(
            src_ref=lat_ref.at[:, pl.ds(pl.multiple_of(target * cols, cols), cols)],
            dst_ref=recv.at[slot],
            send_sem=send_sem.at[d - 1],
            recv_sem=recv_sem.at[d - 1],
            device_id=(group, target),
            device_id_type=MESH,
        )

    def send(d, carry):
        block_copy(d, me).start()
        return carry

    lax.fori_loop(1, n, send, 0)

    fine_weights(k1, k2, km, w1, wlast, wfirst, wnext, w2, wma, wmb)

    p = lax.broadcasted_iota(jnp.int32, (cols, cols), 0)
    w = lax.broadcasted_iota(jnp.int32, (cols, cols), 1)
    half = cols // 2
    perm = (w == jnp.where(p < half, 2 * p, 2 * p - cols + 1)).astype(F32).astype(BF16)
    rows_at = dot_nt(perm, tab_ref[0].astype(F32).astype(BF16)).astype(jnp.int32)
    cols_at = dot_nt(perm, (tab_ref[1] - me * cols).astype(F32).astype(BF16)).astype(jnp.int32)
    wide = per * channels
    lane = lax.broadcasted_iota(jnp.int32, (cols, wide), 1)
    hots = [(cols_at[:, h : h + 1] == w).astype(F32).astype(BF16) for h in range(height)]
    at_row = [jnp.broadcast_to(rows_at[:, h : h + 1], (cols, wide)) - lane // channels for h in range(height)]
    fi = lax.broadcasted_iota(jnp.int32, (per * wide, wide), 0)
    fo = lax.broadcasted_iota(jnp.int32, (per * wide, wide), 1)
    fold = ((fi // wide == fo // channels) & (fi % channels == fo % channels)).astype(F32).astype(BF16)

    mine.wait()

    def receive(d, carry):
        block_copy(d, lax.rem(me - d + n, n)).wait_recv()
        return carry

    lax.fori_loop(1, n, receive, 0)

    def halo(k, src, dst, shift):
        return pltpu.make_async_remote_copy(
            src_ref=src, dst_ref=dst, send_sem=hsend.at[k], recv_sem=hrecv.at[k],
            device_id=(group, lax.rem(me + shift + 2 * n, n)), device_id_type=MESH)

    copies = [
        halo(0, own_ref.at[0], anti_ref, n // 2),
        halo(1, edge.at[1, 0], anti_left_ref, n // 2 + 1),
        halo(2, edge.at[0, 0], anti_right_ref, n // 2 - 1),
        halo(3, edge.at[1], left_ref, 1),
        halo(4, edge.at[0], right_ref, -1),
    ]
    source = recv[...].reshape(n * lat_ref.shape[0], cols)
    tiles = source.shape[0] // wide
    for g in range(own_ref.shape[0]):
        got = dot_nt(jnp.concatenate(hots[g * per : (g + 1) * per], axis=0), source)
        picked = []
        for q in range(per):
            one = jnp.zeros((cols, wide), F32)
            for t in range(tiles):
                value = got[q * cols : (q + 1) * cols, t * wide : (t + 1) * wide]
                one = jnp.where(at_row[g * per + q] == t * per, value, one)
            picked.append(one.astype(BF16))
        block = jnp.dot(jnp.concatenate(picked, axis=1), fold, preferred_element_type=F32)
        own_ref[g] = block.astype(BF16)
        edge[0, g] = jnp.concatenate([block[0:HALO], block[half : half + HALO]], axis=0).astype(BF16)
        edge[1, g] = jnp.concatenate([block[half - HALO : half], block[cols - HALO : cols]], axis=0).astype(BF16)
        if g == 0:
            for c in copies[:3]:
                c.start()

    for c in copies[3:]:
        c.start()

    def sent(d, carry):
        block_copy(d, me).wait_send()
        return carry

    lax.fori_loop(1, n, sent, 0)
    for c in copies:
        c.wait()


def unet_kernel(own_ref, left_ref, right_ref, anti_ref, anti_left_ref, anti_right_ref,
                w1, wlast, wfirst, wnext, w2, wd, wc, wu, wma, wmb, wp, out_ref, xf, x1, x2, x3, xc, xu):
    groups, cols, wide = own_ref.shape
    height = groups * PER
    channels = wide // PER
    half = cols // 2
    J = half + 2 * HALO
    C = w2.shape[0] // 4
    C2 = wd.shape[0]
    COUT = wp.shape[0] // 4
    pairs = height // 2
    AB = pairs + 1

    def spread(g, l, r):
        even = jnp.concatenate([g[:half], r[:HALO], l[:HALO]], axis=0)
        odd = jnp.concatenate([g[half:], r[HALO:], l[HALO:]], axis=0)
        return jnp.concatenate([even, odd, pltpu.roll(even, J - 1, 0), pltpu.roll(odd, 1, 0)], axis=1).astype(BF16)

    for g in range(groups):
        xf[g] = spread(own_ref[g].astype(F32), left_ref[g].astype(F32), right_ref[g].astype(F32))
    xf[groups] = spread(anti_ref[...].astype(F32), anti_left_ref[...].astype(F32), anti_right_ref[...].astype(F32))

    def neighbours(v):
        count = v.shape[0]
        v = v.reshape(count // J, J, v.shape[1])
        lane = lax.broadcasted_iota(jnp.int32, v.shape, 2)
        other = jnp.where(lane < C, pltpu.roll(v, J - 1, 1), pltpu.roll(v, 1, 1))
        return jnp.concatenate([v, other], axis=2).astype(BF16)

    def store_pair(x, i0, count, s):
        x[pl.ds(i0, count), 1] = neighbours(s[:, : 2 * C])
        x[pl.ds(i0 + 1, count), 0] = neighbours(s[:, 2 * C :])

    def wrap(x):
        x[0, 0] = x[AB, 1]
        x[AB, 0] = x[0, 1]
        x[AB - 1, 1] = jnp.zeros(x.shape[2:], BF16)

    def taps(x, i0, count, a, width):
        v = x[pl.ds(i0 + a // 2, count), a % 2, 0:width]
        return v.reshape(count * width, v.shape[-1])

    B = pairs

    def own_loop(steps, body):
        for t in range(steps):
            body(t)

    every = groups + 1
    acc = dot_nt(xf[...].reshape(every * J, 4 * wide), w1[...]).reshape(every, J, PER * 2 * C)
    from_last = dot_nt(xf[pl.ds(0, groups - 1)].reshape((groups - 1) * J, 4 * wide), wlast[...]).reshape(groups - 1, J, 2 * C)
    from_next = dot_nt(xf[pl.ds(1, groups - 1)].reshape((groups - 1) * J, 4 * wide), wnext[...]).reshape(groups - 1, J, 2 * C)
    own_top = dot_nt(xf[groups], wfirst[...])
    anti_top = dot_nt(xf[0], wfirst[...])
    for g in range(every):
        for r in range(PER):
            v = acc[g, :, r * 2 * C : (r + 1) * 2 * C]
            if r == 0:
                v = v + (anti_top if g == groups else own_top if g == 0 else from_last[g - 1])
            if r == PER - 1 and g < groups - 1:
                v = v + from_next[g]
            slot = g * PER + r + 1 + (2 if g == groups else 0)
            if slot // 2 < x1.shape[0]:
                x1[slot // 2, slot % 2] = neighbours(silu(v))[0]
    wrap(x1)

    def second(i0, count):
        acc = dot_nt(taps(x1, i0, count, 0, J), w2[:, : 4 * C])
        for a in range(1, 4):
            acc += dot_nt(taps(x1, i0, count, a, J), w2[:, a * 4 * C : (a + 1) * 4 * C])
        store_pair(x2, i0, count, silu(acc))

    second(AB, 2)
    own_loop(pairs // B, lambda t: second(t * B, B))
    wrap(x2)

    def shifts(v, both):
        v = v.reshape(v.shape[0] // J, J, v.shape[1])
        parts = [v, pltpu.roll(v, J - 1, 1)]
        if both:
            parts.append(pltpu.roll(v, 1, 1))
        return jnp.concatenate(parts, axis=2).astype(BF16)

    def down(i0, slot, count):
        acc = dot_nt(taps(x2, i0, count, 0, J), wd[:, : 4 * C])
        for a in range(1, 3):
            acc += dot_nt(taps(x2, i0, count, a, J), wd[:, a * 4 * C : (a + 1) * 4 * C])
        xc[pl.ds(slot, count)] = shifts(silu(acc), True)

    down(AB, pairs + 3, 2)
    own_loop(pairs // B, lambda t: down(t * B, t * B + 1, B))
    xc[0] = xc[pairs + 3]
    xc[pairs + 2] = xc[1]
    xc[pairs + 1] = jnp.zeros(xc.shape[1:], BF16)

    def coarse(i0, slot, count):
        acc = None
        for a in range(3):
            v = xc[pl.ds(i0 + a, count)].reshape(count * J, 3 * C2)
            part = dot_nt(v, wc[:, a * 3 * C2 : (a + 1) * 3 * C2])
            acc = part if acc is None else acc + part
        xu[pl.ds(slot, count)] = shifts(silu(acc), False)

    coarse(pairs + 2, pairs + 1, 1)
    own_loop(pairs // B, lambda t: coarse(t * B, t * B, B))
    xu[pairs] = jnp.zeros(xu.shape[1:], BF16)

    def up(i0, count):
        acc = dot_nt(xu[pl.ds(i0, count)].reshape(count * J, 2 * C2), wu[:, : 2 * C2])
        return silu(acc + dot_nt(xu[pl.ds(i0 + 1, count)].reshape(count * J, 2 * C2), wu[:, 2 * C2 :]))

    def up_own(t):
        store_pair(x3, t * B, B, up(t * B, B))

    own_loop(pairs // B, up_own)
    v = xu[pairs + 1]
    x3[0, 0] = neighbours(silu(dot_nt(v, wu[0 : 2 * C, : 2 * C2])))[0]
    x3[AB - 1, 1] = jnp.zeros(x3.shape[2:], BF16)

    p = lax.broadcasted_iota(jnp.int32, (cols, cols), 0)
    w = lax.broadcasted_iota(jnp.int32, (cols, cols), 1)
    unperm = (w == jnp.where(p < half, 2 * p, 2 * p - cols + 1)).astype(F32)
    wpb = wp[...].astype(BF16)

    for t in range(pairs // B):
        i0 = t * B
        acc = None
        for a in range(4):
            for x, w in ((x2, wma), (x3, wmb)):
                part = dot_nt(taps(x, i0, B, a, half), w[:, a * 4 * C : (a + 1) * 4 * C])
                acc = part if acc is None else acc + part
        merged = silu(acc).astype(BF16)
        update = dot_nt(wpb, merged)
        lines = []
        plain = [own_ref[g].astype(F32).T for g in range(groups)]
        for b in range(B):
            u = update[:, b * half : (b + 1) * half]
            for q in range(2):
                line = jnp.concatenate([u[2 * q * COUT : (2 * q + 1) * COUT], u[(2 * q + 1) * COUT : (2 * q + 2) * COUT]], axis=1)
                h = 2 * (i0 + b) + q
                at = (h % PER) * channels
                lines.append(line + plain[h // PER][at : at + COUT])
        woven = jnp.dot(jnp.concatenate(lines, axis=0), unperm, precision=lax.Precision.HIGHEST, preferred_element_type=F32)
        for m in range(2 * B):
            out_ref[:, 2 * i0 + m, :] = woven[m * COUT : (m + 1) * COUT]


def shards(latlon, table, k1, k2, kd, kc, ku, km, kp):
    n = lax.axis_size("lon")
    channels, sub_rows, width = latlon.shape
    height, cols = table.shape[1], table.shape[2]
    lat = jnp.swapaxes(latlon, 0, 1).reshape(sub_rows * channels, width)
    vm = pl.BlockSpec(memory_space=pltpu.VMEM)
    groups = height // PER
    edges = jax.ShapeDtypeStruct((groups, 2 * HALO, PER * channels), BF16)
    corner = jax.ShapeDtypeStruct((2 * HALO, PER * channels), BF16)
    C, C2, COUT = k1.shape[2], kd.shape[2], kp.shape[0]
    weights = (
        jax.ShapeDtypeStruct((2 * C * PER, 4 * PER * channels), BF16),
        jax.ShapeDtypeStruct((2 * C, 4 * PER * channels), BF16),
        jax.ShapeDtypeStruct((2 * C, 4 * PER * channels), BF16),
        jax.ShapeDtypeStruct((2 * C, 4 * PER * channels), BF16),
        jax.ShapeDtypeStruct((4 * C, 16 * C), BF16),
        jax.ShapeDtypeStruct((C2, 12 * C), BF16),
        jax.ShapeDtypeStruct((C2, 9 * C2), BF16),
        jax.ShapeDtypeStruct((4 * C, 4 * C2), BF16),
        jax.ShapeDtypeStruct((4 * C, 16 * C), BF16),
        jax.ShapeDtypeStruct((4 * C, 16 * C), BF16),
        jax.ShapeDtypeStruct((4 * COUT, 4 * C), F32),
    )
    ready = pl.pallas_call(
        functools.partial(exchange_kernel, n),
        out_shape=(jax.ShapeDtypeStruct((groups, cols, PER * channels), BF16), edges, edges,
                   jax.ShapeDtypeStruct((cols, PER * channels), BF16), corner, corner) + weights,
        in_specs=[vm] * 9,
        out_specs=(vm,) * 17,
        scratch_shapes=[
            pltpu.VMEM((n, sub_rows * channels, cols), BF16),
            pltpu.VMEM((2, groups, 2 * HALO, PER * channels), BF16),
            pltpu.SemaphoreType.DMA((n - 1,)),
            pltpu.SemaphoreType.DMA((n - 1,)),
            pltpu.SemaphoreType.DMA,
            pltpu.SemaphoreType.DMA((5,)),
            pltpu.SemaphoreType.DMA((5,)),
        ],
        compiler_params=pltpu.CompilerParams(collective_id=0, has_side_effects=True, vmem_limit_bytes=32 * 2**20),
        name="exchange",
    )(lat, table, k1, k2, kd, kc, ku, km, kp)
    J = cols // 2 + 2 * HALO
    pairs = height // 2
    return pl.pallas_call(
        unet_kernel,
        out_shape=jax.ShapeDtypeStruct((COUT, height, cols), F32),
        in_specs=[vm] * 17,
        out_specs=vm,
        scratch_shapes=[
            pltpu.VMEM((height // PER + 1, J, 4 * PER * channels), BF16),
            pltpu.VMEM((pairs + 5, 2, J, 4 * C), BF16),
            pltpu.VMEM((pairs + 4, 2, J, 4 * C), BF16),
            pltpu.VMEM((pairs + 1, 2, J, 4 * C), BF16),
            pltpu.VMEM((pairs + 5, J, 3 * C2), BF16),
            pltpu.VMEM((pairs + 2, J, 2 * C2), BF16),
        ],
        compiler_params=pltpu.CompilerParams(vmem_limit_bytes=32 * 2**20),
        name="unet",
    )(*ready)


def solution(mesh):
    return jax.shard_map(
        shards,
        mesh=mesh,
        in_specs=(P("groups", "lon", None), P(None, None, "lon")) + (P(),) * 7,
        out_specs=P("groups", None, "lon"),
        check_vma=False,
    )
```

profile of v0, /device:TPU:0, one launch (start us, length us, event | category | flops | bytes accessed | tf_op | source)
XLA Modules:
  0.0 27.8 jit_solution(7168100481449448920)
XLA Ops:
  0.0 0.0 copy-start.6
  0.0 0.0 copy-start.3
  0.0 1.0 %copy.10 = bf16[2,16,2048]{2,1,0:T(8,128)(2,1)S(1)} copy(bf16[2,16,2048]{2,0,1:T(2,128)(2,1)} %bitcast.3) | data formatting | bytes 262144 | tf_op jit(solution)/shard_map/transpose | solution.py:348
  1.0 0.0 copy-done.6
  1.0 0.0 copy-start
  1.0 0.1 copy.11.k1
  1.2 0.0 copy-start.1
  1.2 0.0 copy-start.2
  1.2 0.0 copy-start.4
  1.2 0.0 copy-start.5
  1.2 1.2 %copy.12.kd = bf16[3,3,128,64]{3,2,1,0:T(8,128)(2,1)S(1)} copy(bf16[3,3,128,64]{2,3,1,0:T(8,128)(2,1)} %param.13) | data formatting | bytes 294912 | tf_op args[4]
  2.4 0.0 copy-done.3
  2.4 0.0 copy-done
  2.4 0.0 copy-done.1
  2.4 0.0 copy-done.2
  2.4 0.0 copy-done.4
  2.4 0.0 copy-done.5
  2.4 17.2 %exchange.1 = (bf16[4,128,128]{2,1,0:T(8,128)(2,1)S(1)}, bf16[4,16,128]{2,1,0:T(8,128)(2,1)S(1)}, bf16[4,16,128]{2,1,0:T(8,128)(2,1)S(1)}, bf16[128,128]{1,0:T(8...) custom-call(bf16[32,2048]{1,0:T(8,128)(2,1)S(1)} %bitcast.2, ...), custom_call_target="tpu_custom_call" | custom-call | tf_op jit(solution)/shard_map/exchange/pallas_call | solution.py:367
  19.6 8.1 %unet.1 = f32[8,32,128]{2,1,0:T(8,128)} custom-call(bf16[4,128,128]{2,1,0:T(8,128)(2,1)S(1)} %get-tuple-element.22.own_ref, bf16[4,16,128]{2,1,0:T(8,128)(2,1)S(1)} %get-tuple-element.23.left_ref, bf16[4,16,128]{2,1,0:T(8,128)(2,1)S(1)} %get-tuple-element.24.right_ref, bf16[128,128]{1,0:T(8,128)(2,1)S(1)} %get-tuple-element.25.anti_ref, ...), custom_call_target="tpu_custom_call" | custom-call | tf_op jit(solution)/shard_map/unet/pallas_call | solution.py:387
Async XLA Ops:
  0.0 1.0 %copy-start.6 = (bf16[3,3,64,16]{2,3,1,0:T(8,128)(2,1)S(1)}, bf16[3,3,64,16]{2,3,1,0:T(8,128)(2,1)}, u32[]{:S(2)}) copy-start(bf16[3,3,64,16]{2,3,1,0:T(8,128)(2,1)} %param.11) | copy-start | bytes 55300
  0.0 2.4 %copy-start.3 = (bf16[3,3,64,128]{3,2,1,0:T(8,128)(2,1)S(1)}, bf16[3,3,64,128]{3,2,1,0:T(8,128)(2,1)}, u32[]{:S(2)}) copy-start(bf16[3,3,64,128]{3,2,1,0:T(8,128)(2,1)} %km.1) | copy-start | bytes 442372
  1.0 1.4 %copy-start = (bf16[3,3,128,128]{3,2,1,0:T(8,128)(2,1)S(1)}, bf16[3,3,128,128]{3,2,1,0:T(8,128)(2,1)}, u32[]{:S(2)}) copy-start(bf16[3,3,128,128]{3,2,1,0:T(8,128)(2,1)} %kc.1) | copy-start | bytes 884740
  1.2 1.3 %copy-start.1 = (bf16[3,3,64,64]{3,2,1,0:T(8,128)(2,1)S(1)}, bf16[3,3,64,64]{3,2,1,0:T(8,128)(2,1)}, u32[]{:S(2)}) copy-start(bf16[3,3,64,64]{3,2,1,0:T(8,128)(2,1)} %k2.1) | copy-start | bytes 221188
  1.2 1.3 %copy-start.2 = (bf16[3,3,64,128]{3,2,1,0:T(8,128)(2,1)S(1)}, bf16[3,3,64,128]{3,2,1,0:T(8,128)(2,1)}, u32[]{:S(2)}) copy-start(bf16[3,3,64,128]{3,2,1,0:T(8,128)(2,1)} %ku.1) | copy-start | bytes 442372
  1.2 1.3 %copy-start.4 = (s32[2,32,128]{2,1,0:T(8,128)S(1)}, s32[2,32,128]{2,1,0:T(8,128)}, u32[]{:S(2)}) copy-start(s32[2,32,128]{2,1,0:T(8,128)} %tab_ref.1) | copy-start | bytes 98308
  1.2 1.2 %copy-start.5 = (bf16[8,64]{1,0:T(8,128)(2,1)S(1)}, bf16[8,64]{1,0:T(8,128)(2,1)}, u32[]{:S(2)}) copy-start(bf16[8,64]{1,0:T(8,128)(2,1)} %kp.1) | copy-start | bytes 3076
where the time goes:
time: 27.9 us; the launch traced here: 27.8 us
  Pallas kernels  25.3 us (91%)
  local copies, waits for them, and re-layouts  2.35 us (8%)
    pallas_call x1, Pallas kernels, shards(): pl.pallas_call(functools.partial(exchange_kernel, n), out_shape=(jax.Shap...  17.2 us
    pallas_call x1, Pallas kernels, shards(): pl.pallas_call(unet_kernel, out_shape=jax.ShapeDtypeStruct((COUT, height,...  8.12 us
    unnamed x16, local copies, waits for them, and re-layouts  1.37 us
    transpose x1, local copies, waits for them, and re-layouts, shards(): lat = jnp.swapaxes(latlon, 0, 1).reshape(sub_rows * channels, width)  0.98 us

commit v1 on v0

--- a/solution.py
+++ b/solution.py
@@ -23,6 +23,10 @@
 def silu(x):
     half = 0.5 * x
     return half * jnp.tanh(half) + half
+
+
+def dot_nn(a, b):
+    return jnp.dot(a, b, preferred_element_type=F32)
 
 
 def clear(*arrays):
@@ -44,7 +48,7 @@
 
 
 def fine_weights(k1, k2, km, w1, wlast, wfirst, wnext, w2, wma, wmb):
-    C, channels = k1.shape[2], k1.shape[3]
+    channels, C = k1.shape[2], k1.shape[3]
     wide = PER * channels
     clear(w1, wlast, wfirst, wnext, w2, wma, wmb)
     for p in range(2):
@@ -58,23 +62,23 @@
                 for kr in range(3):
                     if 0 <= r + kr - 1 < PER:
                         to = lane + (r + kr - 1) * channels
-                        w1[at : at + C, to : to + channels] = k[kr]
+                        w1[to : to + channels, at : at + C] = k[kr]
             end = lane + (PER - 1) * channels
-            wlast[p * C : (p + 1) * C, end : end + channels] = k[0]
-            wfirst[p * C : (p + 1) * C, lane : lane + channels] = k[0]
-            wnext[p * C : (p + 1) * C, lane : lane + channels] = k[2]
+            wlast[end : end + channels, p * C : (p + 1) * C] = k[0]
+            wfirst[lane : lane + channels, p * C : (p + 1) * C] = k[0]
+            wnext[lane : lane + channels, p * C : (p + 1) * C] = k[2]
     fill(w2, k2, C, 0)
     fill(wma, km, C, 0)
     fill(wmb, km, C, C)
 
 
 def coarse_weights(kd, kc, ku, kp, wd, wc, wu, wp):
-    C2, C = kd.shape[2], kd.shape[3]
+    C, C2 = kd.shape[2], kd.shape[3]
     COUT = kp.shape[0]
     clear(wd, wc, wu, wp)
     for a in range(3):
         for l, kcol in ((0, 1), (1, 2), (3, 0)):
-            wd[:, a * 4 * C + l * C : a * 4 * C + (l + 1) * C] = kd[a, kcol]
+            wd[a * 4 * C + l * C : a * 4 * C + (l + 1) * C] = kd[a, kcol]
         for s, kcol in enumerate((1, 2, 0)):
             wc[:, (a * 3 + s) * C2 : (a * 3 + s + 1) * C2] = kc[a, kcol]
     for q, rows in ((0, ((0, 1),)), (1, ((0, 0), (1, 2)))):
@@ -88,15 +92,16 @@
         wp[g * COUT : (g + 1) * COUT, g * C : (g + 1) * C] = kp[...].astype(F32)
 
 
-def exchange_kernel(n, lat_ref, tab_ref, k1, k2, kd, kc, ku, km, kp,
+def exchange_kernel(n, lat_ref, tab_hbm, k1_hbm, k2_hbm, kd_hbm, kc_hbm, ku_hbm, km_hbm, kp_hbm,
                     own_ref, left_ref, right_ref, anti_ref, anti_left_ref, anti_right_ref,
                     w1, wlast, wfirst, wnext, w2, wd, wc, wu, wma, wmb, wp,
-                    recv, edge, send_sem, recv_sem, own_sem, hsend, hrecv):
+                    tab_ref, k1, k2, kd, kc, ku, km, kp, recv, edge, hot, send_sem, recv_sem, own_sem, hsend, hrecv, load_sem):
     me = lax.axis_index("lon")
     group = lax.axis_index("groups")
-    cols = recv.shape[2]
+    cols = recv.shape[3]
     height = tab_ref.shape[1]
     per = height // own_ref.shape[0]
+    sub_rows = lat_ref.shape[1]
     channels = own_ref.shape[2] // per
     barrier = pltpu.get_barrier_semaphore()
 
@@ -105,15 +110,18 @@
         return carry
 
     lax.fori_loop(1, n, greet, 0)
-    mine = pltpu.make_async_copy(lat_ref.at[:, pl.ds(pl.multiple_of(me * cols, cols), cols)], recv.at[me], own_sem)
+    mine = pltpu.make_async_copy(lat_ref.at[:, :, pl.ds(pl.multiple_of(me * cols, cols), cols)], recv.at[me], own_sem)
     mine.start()
-    coarse_weights(kd, kc, ku, kp, wd, wc, wu, wp)
+    loads = [pltpu.make_async_copy(src, dst, load_sem.at[i]) for i, (src, dst) in enumerate((
+        (tab_hbm, tab_ref), (k1_hbm, k1), (k2_hbm, k2), (kd_hbm, kd), (kc_hbm, kc), (ku_hbm, ku), (km_hbm, km), (kp_hbm, kp)))]
+    for load in loads:
+        load.start()
     pl.semaphore_wait(barrier, n - 1)
 
     def block_copy(d, slot):
         target = lax.rem(me + d, n)
         return pltpu.make_async_remote_copy(
-            src_ref=lat_ref.at[:, pl.ds(pl.multiple_of(target * cols, cols), cols)],
+            src_ref=lat_ref.at[:, :, pl.ds(pl.multiple_of(target * cols, cols), cols)],
             dst_ref=recv.at[slot],
             send_sem=send_sem.at[d - 1],
             recv_sem=recv_sem.at[d - 1],
@@ -127,8 +135,7 @@
 
     lax.fori_loop(1, n, send, 0)
 
-    fine_weights(k1, k2, km, w1, wlast, wfirst, wnext, w2, wma, wmb)
-
+    loads[0].wait()
     p = lax.broadcasted_iota(jnp.int32, (cols, cols), 0)
     w = lax.broadcasted_iota(jnp.int32, (cols, cols), 1)
     half = cols // 2
@@ -137,11 +144,23 @@
     cols_at = dot_nt(perm, (tab_ref[1] - me * cols).astype(F32).astype(BF16)).astype(jnp.int32)
     wide = per * channels
     lane = lax.broadcasted_iota(jnp.int32, (cols, wide), 1)
-    hots = [(cols_at[:, h : h + 1] == w).astype(F32).astype(BF16) for h in range(height)]
-    at_row = [jnp.broadcast_to(rows_at[:, h : h + 1], (cols, wide)) - lane // channels for h in range(height)]
+    wide_hot = lax.broadcasted_iota(jnp.int32, (cols, 2 * cols), 1)
+    held = sub_rows * channels
+    per_tile = wide // held
+    spot = lane // held * sub_rows + lane % sub_rows
+    pair = rows_at // (2 * sub_rows)
+    col_key = cols_at + rows_at // sub_rows % 2 * cols
+    row_key = pair * sub_rows + rows_at % sub_rows
+    for h in range(height):
+        hot[h * cols : (h + 1) * cols] = (col_key[:, h : h + 1] == wide_hot).astype(F32).astype(BF16)
+    at_row = [jnp.broadcast_to(row_key[:, h : h + 1], (cols, wide)) - spot for h in range(height)]
     fi = lax.broadcasted_iota(jnp.int32, (per * wide, wide), 0)
     fo = lax.broadcasted_iota(jnp.int32, (per * wide, wide), 1)
-    fold = ((fi // wide == fo // channels) & (fi % channels == fo % channels)).astype(F32).astype(BF16)
+    fold = ((fi // wide == fo // channels) & (fi % held // sub_rows == fo % channels)).astype(F32).astype(BF16)
+    for load in loads[1:]:
+        load.wait()
+    coarse_weights(kd, kc, ku, kp, wd, wc, wu, wp)
+    fine_weights(k1, k2, km, w1, wlast, wfirst, wnext, w2, wma, wmb)
 
     mine.wait()
 
@@ -163,16 +182,17 @@
         halo(3, edge.at[1], left_ref, 1),
         halo(4, edge.at[0], right_ref, -1),
     ]
-    source = recv[...].reshape(n * lat_ref.shape[0], cols)
+    arrived = recv[...].reshape(n // 2, 2, held, cols)
+    source = jnp.concatenate([arrived[:, 0], arrived[:, 1]], axis=2).reshape(n // 2 * held, 2 * cols)
     tiles = source.shape[0] // wide
     for g in range(own_ref.shape[0]):
-        got = dot_nt(jnp.concatenate(hots[g * per : (g + 1) * per], axis=0), source)
+        got = dot_nt(hot[g * per * cols : (g + 1) * per * cols], source)
         picked = []
         for q in range(per):
             one = jnp.zeros((cols, wide), F32)
             for t in range(tiles):
                 value = got[q * cols : (q + 1) * cols, t * wide : (t + 1) * wide]
-                one = jnp.where(at_row[g * per + q] == t * per, value, one)
+                one = jnp.where(at_row[g * per + q] == t * per_tile * sub_rows, value, one)
             picked.append(one.astype(BF16))
         block = jnp.dot(jnp.concatenate(picked, axis=1), fold, preferred_element_type=F32)
         own_ref[g] = block.astype(BF16)
@@ -202,7 +222,7 @@
     half = cols // 2
     J = half + 2 * HALO
     C = w2.shape[0] // 4
-    C2 = wd.shape[0]
+    C2 = wd.shape[1]
     COUT = wp.shape[0] // 4
     pairs = height // 2
     AB = pairs + 1
@@ -243,11 +263,11 @@
             body(t)
 
     every = groups + 1
-    acc = dot_nt(xf[...].reshape(every * J, 4 * wide), w1[...]).reshape(every, J, PER * 2 * C)
-    from_last = dot_nt(xf[pl.ds(0, groups - 1)].reshape((groups - 1) * J, 4 * wide), wlast[...]).reshape(groups - 1, J, 2 * C)
-    from_next = dot_nt(xf[pl.ds(1, groups - 1)].reshape((groups - 1) * J, 4 * wide), wnext[...]).reshape(groups - 1, J, 2 * C)
-    own_top = dot_nt(xf[groups], wfirst[...])
-    anti_top = dot_nt(xf[0], wfirst[...])
+    acc = dot_nn(xf[...].reshape(every * J, 4 * wide), w1[...]).reshape(every, J, PER * 2 * C)
+    from_last = dot_nn(xf[pl.ds(0, groups - 1)].reshape((groups - 1) * J, 4 * wide), wlast[...]).reshape(groups - 1, J, 2 * C)
+    from_next = dot_nn(xf[pl.ds(1, groups - 1)].reshape((groups - 1) * J, 4 * wide), wnext[...]).reshape(groups - 1, J, 2 * C)
+    own_top = dot_nn(xf[groups], wfirst[...])
+    anti_top = dot_nn(xf[0], wfirst[...])
     for g in range(every):
         for r in range(PER):
             v = acc[g, :, r * 2 * C : (r + 1) * 2 * C]
@@ -278,9 +298,9 @@
         return jnp.concatenate(parts, axis=2).astype(BF16)
 
     def down(i0, slot, count):
-        acc = dot_nt(taps(x2, i0, count, 0, J), wd[:, : 4 * C])
+        acc = dot_nn(taps(x2, i0, count, 0, J), wd[: 4 * C])
         for a in range(1, 3):
-            acc += dot_nt(taps(x2, i0, count, a, J), wd[:, a * 4 * C : (a + 1) * 4 * C])
+            acc += dot_nn(taps(x2, i0, count, a, J), wd[a * 4 * C : (a + 1) * 4 * C])
         xc[pl.ds(slot, count)] = shifts(silu(acc), True)
 
     down(AB, pairs + 3, 2)
@@ -343,21 +363,21 @@
 
 def shards(latlon, table, k1, k2, kd, kc, ku, km, kp):
     n = lax.axis_size("lon")
+    k1, kd = jnp.swapaxes(k1, 2, 3), jnp.swapaxes(kd, 2, 3)
     channels, sub_rows, width = latlon.shape
     height, cols = table.shape[1], table.shape[2]
-    lat = jnp.swapaxes(latlon, 0, 1).reshape(sub_rows * channels, width)
     vm = pl.BlockSpec(memory_space=pltpu.VMEM)
     groups = height // PER
     edges = jax.ShapeDtypeStruct((groups, 2 * HALO, PER * channels), BF16)
     corner = jax.ShapeDtypeStruct((2 * HALO, PER * channels), BF16)
-    C, C2, COUT = k1.shape[2], kd.shape[2], kp.shape[0]
+    C, C2, COUT = k1.shape[3], kd.shape[3], kp.shape[0]
     weights = (
-        jax.ShapeDtypeStruct((2 * C * PER, 4 * PER * channels), BF16),
-        jax.ShapeDtypeStruct((2 * C, 4 * PER * channels), BF16),
-        jax.ShapeDtypeStruct((2 * C, 4 * PER * channels), BF16),
-        jax.ShapeDtypeStruct((2 * C, 4 * PER * channels), BF16),
+        jax.ShapeDtypeStruct((4 * PER * channels, 2 * C * PER), BF16),
+        jax.ShapeDtypeStruct((4 * PER * channels, 2 * C), BF16),
+        jax.ShapeDtypeStruct((4 * PER * channels, 2 * C), BF16),
+        jax.ShapeDtypeStruct((4 * PER * channels, 2 * C), BF16),
         jax.ShapeDtypeStruct((4 * C, 16 * C), BF16),
-        jax.ShapeDtypeStruct((C2, 12 * C), BF16),
+        jax.ShapeDtypeStruct((12 * C, C2), BF16),
         jax.ShapeDtypeStruct((C2, 9 * C2), BF16),
         jax.ShapeDtypeStruct((4 * C, 4 * C2), BF16),
         jax.ShapeDtypeStruct((4 * C, 16 * C), BF16),
@@ -368,20 +388,24 @@
         functools.partial(exchange_kernel, n),
         out_shape=(jax.ShapeDtypeStruct((groups, cols, PER * channels), BF16), edges, edges,
                    jax.ShapeDtypeStruct((cols, PER * channels), BF16), corner, corner) + weights,
-        in_specs=[vm] * 9,
+        in_specs=[pl.BlockSpec(memory_space=pltpu.HBM)] * 9,
         out_specs=(vm,) * 17,
         scratch_shapes=[
-            pltpu.VMEM((n, sub_rows * channels, cols), BF16),
+            pltpu.VMEM(table.shape, table.dtype),
+        ] + [pltpu.VMEM(k.shape, BF16) for k in (k1, k2, kd, kc, ku, km, kp)] + [
+            pltpu.VMEM((n, channels, sub_rows, cols), BF16),
             pltpu.VMEM((2, groups, 2 * HALO, PER * channels), BF16),
+            pltpu.VMEM((height * cols, 2 * cols), BF16),
             pltpu.SemaphoreType.DMA((n - 1,)),
             pltpu.SemaphoreType.DMA((n - 1,)),
             pltpu.SemaphoreType.DMA,
             pltpu.SemaphoreType.DMA((5,)),
             pltpu.SemaphoreType.DMA((5,)),
+            pltpu.SemaphoreType.DMA((8,)),
         ],
         compiler_params=pltpu.CompilerParams(collective_id=0, has_side_effects=True, vmem_limit_bytes=32 * 2**20),
         name="exchange",
-    )(lat, table, k1, k2, kd, kc, ku, km, kp)
+    )(*(pltpu.with_memory_space_constraint(v, pltpu.HBM) for v in (latlon, table, k1, k2, kd, kc, ku, km, kp)))
     J = cols // 2 + 2 * HALO
     pairs = height // 2
     return pl.pallas_call(

time: 27.9 us -> 25.6 us (0.918)
  local copies, waits for them, and re-layouts: 2.35 us -> 0 us
    unnamed x16 -> x0, local copies, waits for them, and re-layouts: 1.37 us -> none
    transpose x1 -> x0, local copies, waits for them, and re-layouts: 0.98 us -> none  [shards(): lat = jnp.swapaxes(latlon, 0, 1).reshape(sub_rows * channels, width)]
where the time goes in v1:
time: 25.6 us; the launch traced here: 25.4 us
  Pallas kernels  25.4 us (99%)
    pallas_call x1, Pallas kernels, shards(): pl.pallas_call(functools.partial(exchange_kernel, n), out_shape=(jax.Shap...  17.4 us
    pallas_call x1, Pallas kernels, shards(): pl.pallas_call(unet_kernel, out_shape=jax.ShapeDtypeStruct((COUT, height,...  8.06 us

profile of v1, /device:TPU:0, one launch (start us, length us, event | category | flops | bytes accessed | tf_op | source)
XLA Modules:
  0.0 25.4 jit_solution(14114505339998394416)
XLA Ops:
  0.0 17.4 %exchange.1 = (bf16[4,128,128]{2,1,0:T(8,128)(2,1)S(1)}, bf16[4,16,128]{2,1,0:T(8,128)(2,1)S(1)}, bf16[4,16,128]{2,1,0:T(8,128)(2,1)S(1)}, bf16[128,128]{1,0:T(8...) custom-call(bf16[16,2,2048]{2,1,0:T(2,128)(2,1)} %lat_ref.1, ...), custom_call_target="tpu_custom_call" | custom-call | tf_op jit(solution)/shard_map/exchange/pallas_call | solution.py:387
  17.4 8.1 %unet.1 = f32[8,32,128]{2,1,0:T(8,128)} custom-call(bf16[4,128,128]{2,1,0:T(8,128)(2,1)S(1)} %get-tuple-element.22.own_ref, bf16[4,16,128]{2,1,0:T(8,128)(2,1)S(1)} %get-tuple-element.23.left_ref, bf16[4,16,128]{2,1,0:T(8,128)(2,1)S(1)} %get-tuple-element.24.right_ref, bf16[128,128]{1,0:T(8,128)(2,1)S(1)} %get-tuple-element.25.anti_ref, ...), custom_call_target="tpu_custom_call" | custom-call | tf_op jit(solution)/shard_map/unet/pallas_call | solution.py:411

commit v2 on v1

--- a/solution.py
+++ b/solution.py
@@ -10,7 +10,7 @@
 MESH = pl.DeviceIdType.MESH
 F32 = jnp.float32
 BF16 = jnp.bfloat16
-HALO = 8
+HALO = 4
 PER = 8
 OFFSETS = (0, 1, 2, -1)
 NT = (((1,), (1,)), ((), ()))
@@ -93,9 +93,9 @@
 
 
 def exchange_kernel(n, lat_ref, tab_hbm, k1_hbm, k2_hbm, kd_hbm, kc_hbm, ku_hbm, km_hbm, kp_hbm,
-                    own_ref, left_ref, right_ref, anti_ref, anti_left_ref, anti_right_ref,
-                    w1, wlast, wfirst, wnext, w2, wd, wc, wu, wma, wmb, wp,
-                    tab_ref, k1, k2, kd, kc, ku, km, kp, recv, edge, hot, send_sem, recv_sem, own_sem, hsend, hrecv, load_sem):
+                    own_ref, halo_ref, w1, wlast, wfirst, wnext, w2, wd, wc, wu, wma, wmb, wp,
+                    tab_ref, k1, k2, kd, kc, ku, km, kp, recv, edge, hot, edge_hot,
+                    send_sem, recv_sem, own_sem, hsend, hrecv, load_sem):
     me = lax.axis_index("lon")
     group = lax.axis_index("groups")
     cols = recv.shape[3]
@@ -123,8 +123,8 @@
         return pltpu.make_async_remote_copy(
             src_ref=lat_ref.at[:, :, pl.ds(pl.multiple_of(target * cols, cols), cols)],
             dst_ref=recv.at[slot],
-            send_sem=send_sem.at[d - 1],
-            recv_sem=recv_sem.at[d - 1],
+            send_sem=send_sem,
+            recv_sem=recv_sem,
             device_id=(group, target),
             device_id_type=MESH,
         )
@@ -151,6 +151,26 @@
     pair = rows_at // (2 * sub_rows)
     col_key = cols_at + rows_at // sub_rows % 2 * cols
     row_key = pair * sub_rows + rows_at % sub_rows
+    groups = own_ref.shape[0]
+    strip = 2 * HALO
+    ep = lax.broadcasted_iota(jnp.int32, (2 * strip, cols), 0)
+    ew = lax.broadcasted_iota(jnp.int32, (2 * strip, cols), 1)
+    first = jnp.where(ep < HALO, 2 * ep, 2 * (ep - HALO) + 1)
+    last = jnp.where(ep < strip + HALO, 2 * (ep - strip) + 1, 2 * (ep - strip - HALO)) + cols - strip
+    edge_perm = (ew == jnp.where(ep < strip, first, last)).astype(F32).astype(BF16)
+    edge_rows = dot_nt(edge_perm, tab_ref[0].astype(F32).astype(BF16)).astype(jnp.int32)
+    edge_cols = dot_nt(edge_perm, (tab_ref[1] - me * cols).astype(F32).astype(BF16)).astype(jnp.int32)
+    edge_col_key = edge_cols + edge_rows // sub_rows % 2 * cols
+    edge_row_key = edge_rows // (2 * sub_rows) * sub_rows + edge_rows % sub_rows
+    edge_held = 2 * groups * strip
+
+    def edge_of(keys, q, width):
+        return jnp.concatenate([jnp.broadcast_to(keys[side * strip : (side + 1) * strip, g * per + q : g * per + q + 1], (strip, width))
+                                for side in range(2) for g in range(groups)], axis=0)
+
+    for q in range(per):
+        edge_hot[q * edge_held : (q + 1) * edge_held] = (edge_of(edge_col_key, q, 2 * cols) == wide_hot[:edge_held]).astype(F32).astype(BF16)
+    edge_at = [edge_of(edge_row_key, q, wide) - spot[:edge_held] for q in range(per)]
     for h in range(height):
         hot[h * cols : (h + 1) * cols] = (col_key[:, h : h + 1] == wide_hot).astype(F32).astype(BF16)
     at_row = [jnp.broadcast_to(row_key[:, h : h + 1], (cols, wide)) - spot for h in range(height)]
@@ -164,58 +184,51 @@
 
     mine.wait()
 
-    def receive(d, carry):
-        block_copy(d, lax.rem(me - d + n, n)).wait_recv()
-        return carry
-
-    lax.fori_loop(1, n, receive, 0)
-
-    def halo(k, src, dst, shift):
+    blocks = pltpu.make_async_remote_copy(
+        src_ref=recv.at[pl.ds(0, n - 1)], dst_ref=recv.at[pl.ds(0, n - 1)], send_sem=send_sem, recv_sem=recv_sem,
+        device_id=(group, lax.rem(me + 1, n)), device_id_type=MESH)
+    blocks.wait_recv()
+
+    def halo(src, dst, shift):
         return pltpu.make_async_remote_copy(
-            src_ref=src, dst_ref=dst, send_sem=hsend.at[k], recv_sem=hrecv.at[k],
+            src_ref=src, dst_ref=dst, send_sem=hsend, recv_sem=hrecv,
             device_id=(group, lax.rem(me + shift + 2 * n, n)), device_id_type=MESH)
 
-    copies = [
-        halo(0, own_ref.at[0], anti_ref, n // 2),
-        halo(1, edge.at[1, 0], anti_left_ref, n // 2 + 1),
-        halo(2, edge.at[0, 0], anti_right_ref, n // 2 - 1),
-        halo(3, edge.at[1], left_ref, 1),
-        halo(4, edge.at[0], right_ref, -1),
-    ]
+    lead = groups * strip
+    firsts, lasts = edge.at[pl.ds(0, lead)], edge.at[pl.ds(lead, lead)]
     arrived = recv[...].reshape(n // 2, 2, held, cols)
     source = jnp.concatenate([arrived[:, 0], arrived[:, 1]], axis=2).reshape(n // 2 * held, 2 * cols)
     tiles = source.shape[0] // wide
-    for g in range(own_ref.shape[0]):
+
+    def pick(got, at, q, count):
+        one = jnp.zeros((count, wide), F32)
+        for t in range(tiles):
+            value = got[q * count : (q + 1) * count, t * wide : (t + 1) * wide]
+            one = jnp.where(at == t * per_tile * sub_rows, value, one)
+        return one.astype(BF16)
+
+    got = dot_nt(edge_hot[...], source)
+    picked = [pick(got, edge_at[q], q, edge_held) for q in range(per)]
+    edge[...] = jnp.dot(jnp.concatenate(picked, axis=1), fold, preferred_element_type=F32).astype(BF16)
+    for src, first_row, count, shift in (
+        (lasts, cols + 4 * strip, lead, 1), (firsts, cols + 4 * strip + lead, lead, -1),
+        (edge.at[pl.ds(lead, 2 * strip)], cols, 2 * strip, n // 2 + 1), (edge.at[pl.ds(0, 2 * strip)], cols + 2 * strip, 2 * strip, n // 2 - 1),
+    ):
+        halo(src, halo_ref.at[pl.ds(first_row, count)], shift).start()
+    for g in range(groups):
         got = dot_nt(hot[g * per * cols : (g + 1) * per * cols], source)
-        picked = []
-        for q in range(per):
-            one = jnp.zeros((cols, wide), F32)
-            for t in range(tiles):
-                value = got[q * cols : (q + 1) * cols, t * wide : (t + 1) * wide]
-                one = jnp.where(at_row[g * per + q] == t * per_tile * sub_rows, value, one)
-            picked.append(one.astype(BF16))
-        block = jnp.dot(jnp.concatenate(picked, axis=1), fold, preferred_element_type=F32)
-        own_ref[g] = block.astype(BF16)
-        edge[0, g] = jnp.concatenate([block[0:HALO], block[half : half + HALO]], axis=0).astype(BF16)
-        edge[1, g] = jnp.concatenate([block[half - HALO : half], block[cols - HALO : cols]], axis=0).astype(BF16)
+        picked = [pick(got, at_row[g * per + q], q, cols) for q in range(per)]
+        own_ref[g] = jnp.dot(jnp.concatenate(picked, axis=1), fold, preferred_element_type=F32).astype(BF16)
         if g == 0:
-            for c in copies[:3]:
-                c.start()
-
-    for c in copies[3:]:
-        c.start()
-
-    def sent(d, carry):
-        block_copy(d, me).wait_send()
-        return carry
-
-    lax.fori_loop(1, n, sent, 0)
-    for c in copies:
-        c.wait()
-
-
-def unet_kernel(own_ref, left_ref, right_ref, anti_ref, anti_left_ref, anti_right_ref,
-                w1, wlast, wfirst, wnext, w2, wd, wc, wu, wma, wmb, wp, out_ref, xf, x1, x2, x3, xc, xu):
+            halo(own_ref.at[0], halo_ref.at[pl.ds(0, cols)], n // 2).start()
+
+    blocks.wait_send()
+    every = halo(halo_ref, halo_ref, 1)
+    every.wait_send()
+    every.wait_recv()
+
+
+def unet_kernel(own_ref, halo_ref, w1, wlast, wfirst, wnext, w2, wd, wc, wu, wma, wmb, wp, out_ref, xf, x1, x2, x3, xc, xu):
     groups, cols, wide = own_ref.shape
     height = groups * PER
     channels = wide // PER
@@ -227,14 +240,19 @@
     pairs = height // 2
     AB = pairs + 1
 
+    strip = 2 * HALO
+    upper = lax.broadcasted_iota(jnp.int32, (strip, wide), 0) < HALO
+
     def spread(g, l, r):
-        even = jnp.concatenate([g[:half], r[:HALO], l[:HALO]], axis=0)
-        odd = jnp.concatenate([g[half:], r[HALO:], l[HALO:]], axis=0)
+        even = jnp.concatenate([g[:half], jnp.where(upper, r, l)], axis=0)
+        odd = jnp.concatenate([g[half:], pltpu.roll(jnp.where(upper, l, r), HALO, 0)], axis=0)
         return jnp.concatenate([even, odd, pltpu.roll(even, J - 1, 0), pltpu.roll(odd, 1, 0)], axis=1).astype(BF16)
 
+    around = halo_ref[...].astype(F32)
+    corners, sides = around[cols : cols + 4 * strip], around[cols + 4 * strip :]
     for g in range(groups):
-        xf[g] = spread(own_ref[g].astype(F32), left_ref[g].astype(F32), right_ref[g].astype(F32))
-    xf[groups] = spread(anti_ref[...].astype(F32), anti_left_ref[...].astype(F32), anti_right_ref[...].astype(F32))
+        xf[g] = spread(own_ref[g].astype(F32), sides[g * strip : (g + 1) * strip], sides[(groups + g) * strip : (groups + g + 1) * strip])
+    xf[groups] = spread(around[:cols], corners[:strip], corners[2 * strip : 3 * strip])
 
     def neighbours(v):
         count = v.shape[0]
@@ -256,7 +274,8 @@
         v = x[pl.ds(i0 + a // 2, count), a % 2, 0:width]
         return v.reshape(count * width, v.shape[-1])
 
-    B = pairs
+    B = 8
+    BM = 4
 
     def own_loop(steps, body):
         for t in range(steps):
@@ -281,9 +300,7 @@
     wrap(x1)
 
     def second(i0, count):
-        acc = dot_nt(taps(x1, i0, count, 0, J), w2[:, : 4 * C])
-        for a in range(1, 4):
-            acc += dot_nt(taps(x1, i0, count, a, J), w2[:, a * 4 * C : (a + 1) * 4 * C])
+        acc = dot_nt(jnp.concatenate([taps(x1, i0, count, a, J) for a in range(4)], axis=1), w2[...])
         store_pair(x2, i0, count, silu(acc))
 
     second(AB, 2)
@@ -298,9 +315,7 @@
         return jnp.concatenate(parts, axis=2).astype(BF16)
 
     def down(i0, slot, count):
-        acc = dot_nn(taps(x2, i0, count, 0, J), wd[: 4 * C])
-        for a in range(1, 3):
-            acc += dot_nn(taps(x2, i0, count, a, J), wd[a * 4 * C : (a + 1) * 4 * C])
+        acc = dot_nn(jnp.concatenate([taps(x2, i0, count, a, J) for a in range(3)], axis=1), wd[...])
         xc[pl.ds(slot, count)] = shifts(silu(acc), True)
 
     down(AB, pairs + 3, 2)
@@ -310,11 +325,7 @@
     xc[pairs + 1] = jnp.zeros(xc.shape[1:], BF16)
 
     def coarse(i0, slot, count):
-        acc = None
-        for a in range(3):
-            v = xc[pl.ds(i0 + a, count)].reshape(count * J, 3 * C2)
-            part = dot_nt(v, wc[:, a * 3 * C2 : (a + 1) * 3 * C2])
-            acc = part if acc is None else acc + part
+        acc = dot_nt(jnp.concatenate([xc[pl.ds(i0 + a, count)].reshape(count * J, 3 * C2) for a in range(3)], axis=1), wc[...])
         xu[pl.ds(slot, count)] = shifts(silu(acc), False)
 
     coarse(pairs + 2, pairs + 1, 1)
@@ -322,8 +333,7 @@
     xu[pairs] = jnp.zeros(xu.shape[1:], BF16)
 
     def up(i0, count):
-        acc = dot_nt(xu[pl.ds(i0, count)].reshape(count * J, 2 * C2), wu[:, : 2 * C2])
-        return silu(acc + dot_nt(xu[pl.ds(i0 + 1, count)].reshape(count * J, 2 * C2), wu[:, 2 * C2 :]))
+        return silu(dot_nt(jnp.concatenate([xu[pl.ds(i0 + a, count)].reshape(count * J, 2 * C2) for a in range(2)], axis=1), wu[...]))
 
     def up_own(t):
         store_pair(x3, t * B, B, up(t * B, B))
@@ -335,30 +345,32 @@
 
     p = lax.broadcasted_iota(jnp.int32, (cols, cols), 0)
     w = lax.broadcasted_iota(jnp.int32, (cols, cols), 1)
-    unperm = (w == jnp.where(p < half, 2 * p, 2 * p - cols + 1)).astype(F32)
+    unperm = (w == jnp.where(p < half, 2 * p, 2 * p - cols + 1)).astype(F32).astype(BF16)
+    unperm = jnp.concatenate([unperm, unperm], axis=0)
     wpb = wp[...].astype(BF16)
-
-    for t in range(pairs // B):
-        i0 = t * B
-        acc = None
-        for a in range(4):
-            for x, w in ((x2, wma), (x3, wmb)):
-                part = dot_nt(taps(x, i0, B, a, half), w[:, a * 4 * C : (a + 1) * 4 * C])
-                acc = part if acc is None else acc + part
-        merged = silu(acc).astype(BF16)
-        update = dot_nt(wpb, merged)
-        lines = []
-        plain = [own_ref[g].astype(F32).T for g in range(groups)]
-        for b in range(B):
+    plain = [own_ref[g].astype(F32).T for g in range(groups)]
+
+    def merge(i0, count):
+        tiles = [taps(x, i0, count, a, half) for x in (x2, x3) for a in range(4)]
+        return silu(dot_nt(jnp.concatenate(tiles, axis=1), jnp.concatenate([wma[...], wmb[...]], axis=1))).astype(BF16)
+
+    merged = [merge(t * BM, BM) for t in range(pairs // BM)]
+    lines = []
+    for t in range(pairs // BM):
+        update = dot_nt(wpb, merged[t])
+        for b in range(BM):
             u = update[:, b * half : (b + 1) * half]
             for q in range(2):
                 line = jnp.concatenate([u[2 * q * COUT : (2 * q + 1) * COUT], u[(2 * q + 1) * COUT : (2 * q + 2) * COUT]], axis=1)
-                h = 2 * (i0 + b) + q
+                h = 2 * (t * BM + b) + q
                 at = (h % PER) * channels
                 lines.append(line + plain[h // PER][at : at + COUT])
-        woven = jnp.dot(jnp.concatenate(lines, axis=0), unperm, precision=lax.Precision.HIGHEST, preferred_element_type=F32)
-        for m in range(2 * B):
-            out_ref[:, 2 * i0 + m, :] = woven[m * COUT : (m + 1) * COUT]
+    lines = jnp.concatenate(lines, axis=0)
+    high = lines.astype(BF16)
+    low = (lines - high.astype(F32)).astype(BF16)
+    woven = dot_nn(jnp.concatenate([high, low], axis=1), unperm)
+    for h in range(height):
+        out_ref[:, h, :] = woven[h * COUT : (h + 1) * COUT]
 
 
 def shards(latlon, table, k1, k2, kd, kc, ku, km, kp):
@@ -368,8 +380,8 @@
     height, cols = table.shape[1], table.shape[2]
     vm = pl.BlockSpec(memory_space=pltpu.VMEM)
     groups = height // PER
-    edges = jax.ShapeDtypeStruct((groups, 2 * HALO, PER * channels), BF16)
-    corner = jax.ShapeDtypeStruct((2 * HALO, PER * channels), BF16)
+    sides = 2 * groups * 2 * HALO
+    around = jax.ShapeDtypeStruct((cols + 8 * HALO + sides, PER * channels), BF16)
     C, C2, COUT = k1.shape[3], kd.shape[3], kp.shape[0]
     weights = (
         jax.ShapeDtypeStruct((4 * PER * channels, 2 * C * PER), BF16),
@@ -386,21 +398,21 @@
     )
     ready = pl.pallas_call(
         functools.partial(exchange_kernel, n),
-        out_shape=(jax.ShapeDtypeStruct((groups, cols, PER * channels), BF16), edges, edges,
-                   jax.ShapeDtypeStruct((cols, PER * channels), BF16), corner, corner) + weights,
+        out_shape=(jax.ShapeDtypeStruct((groups, cols, PER * channels), BF16), around) + weights,
         in_specs=[pl.BlockSpec(memory_space=pltpu.HBM)] * 9,
-        out_specs=(vm,) * 17,
+        out_specs=(vm,) * 13,
         scratch_shapes=[
             pltpu.VMEM(table.shape, table.dtype),
         ] + [pltpu.VMEM(k.shape, BF16) for k in (k1, k2, kd, kc, ku, km, kp)] + [
             pltpu.VMEM((n, channels, sub_rows, cols), BF16),
-            pltpu.VMEM((2, groups, 2 * HALO, PER * channels), BF16),
+            pltpu.VMEM((sides, PER * channels), BF16),
             pltpu.VMEM((height * cols, 2 * cols), BF16),
-            pltpu.SemaphoreType.DMA((n - 1,)),
-            pltpu.SemaphoreType.DMA((n - 1,)),
+            pltpu.VMEM((PER * sides, 2 * cols), BF16),
             pltpu.SemaphoreType.DMA,
-            pltpu.SemaphoreType.DMA((5,)),
-            pltpu.SemaphoreType.DMA((5,)),
+            pltpu.SemaphoreType.DMA,
+            pltpu.SemaphoreType.DMA,
+            pltpu.SemaphoreType.DMA,
+            pltpu.SemaphoreType.DMA,
             pltpu.SemaphoreType.DMA((8,)),
         ],
         compiler_params=pltpu.CompilerParams(collective_id=0, has_side_effects=True, vmem_limit_bytes=32 * 2**20),
@@ -411,7 +423,7 @@
     return pl.pallas_call(
         unet_kernel,
         out_shape=jax.ShapeDtypeStruct((COUT, height, cols), F32),
-        in_specs=[vm] * 17,
+        in_specs=[vm] * 13,
         out_specs=vm,
         scratch_shapes=[
             pltpu.VMEM((height // PER + 1, J, 4 * PER * channels), BF16),

time: 25.6 us -> 22.1 us (0.86)
  Pallas kernels: 25.4 us -> 21.9 us
    pallas_call x1, Pallas kernels: 8.06 us -> 5.91 us  [shards(): pl.pallas_call(unet_kernel, out_shape=jax.ShapeDtypeStruct((COUT, height,...]
    pallas_call x1, Pallas kernels: 17.4 us -> 16 us  [shards(): pl.pallas_call(functools.partial(exchange_kernel, n), out_shape=(jax.Shap...]
where the time goes in v2:
time: 22.1 us; the launch traced here: 21.9 us
  Pallas kernels  21.9 us (99%)
    pallas_call x1, Pallas kernels, shards(): pl.pallas_call(functools.partial(exchange_kernel, n), out_shape=(jax.Shap...  16 us
    pallas_call x1, Pallas kernels, shards(): pl.pallas_call(unet_kernel, out_shape=jax.ShapeDtypeStruct((COUT, height,...  5.91 us

profile of v2, /device:TPU:0, one launch (start us, length us, event | category | flops | bytes accessed | tf_op | source)
XLA Modules:
  0.0 21.9 jit_solution(17030587097409818390)
XLA Ops:
  0.0 16.0 %exchange.1 = (bf16[4,128,128]{2,1,0:T(8,128)(2,1)S(1)}, bf16[224,128]{1,0:T(8,128)(2,1)S(1)}, bf16[512,1024]{1,0:T(8,128)(2,1)S(1)}, bf16[512,128]{1,0:T(8,128)...) custom-call(bf16[16,2,2048]{2,1,0:T(2,128)(2,1)} %lat_ref.1, ...), custom_call_target="tpu_custom_call" | custom-call | tf_op jit(solution)/shard_map/exchange/pallas_call | solution.py:399
  16.0 5.9 %unet.1 = f32[8,32,128]{2,1,0:T(8,128)} custom-call(bf16[4,128,128]{2,1,0:T(8,128)(2,1)S(1)} %get-tuple-element.18.own_ref, bf16[224,128]{1,0:T(8,128)(2,1)S(1)} %get-tuple-element.19.halo_ref, bf16[512,1024]{1,0:T(8,128)(2,1)S(1)} %get-tuple-element.20.w1, bf16[512,128]{1,0:T(8,128)(2,1)S(1)} %get-tuple-element.21.wlast, ...), custom_call_target="tpu_custom_call" | custom-call | tf_op jit(solution)/shard_map/unet/pallas_call | solution.py:423

commit v3 on v2

--- a/solution.py
+++ b/solution.py
@@ -94,7 +94,7 @@
 
 def exchange_kernel(n, lat_ref, tab_hbm, k1_hbm, k2_hbm, kd_hbm, kc_hbm, ku_hbm, km_hbm, kp_hbm,
                     own_ref, halo_ref, w1, wlast, wfirst, wnext, w2, wd, wc, wu, wma, wmb, wp,
-                    tab_ref, k1, k2, kd, kc, ku, km, kp, recv, edge, hot, edge_hot,
+                    tab_ref, k1, k2, kd, kc, ku, km, kp, recv, edge, hot, edge_hot, edge_at, at_ref, fold_ref,
                     send_sem, recv_sem, own_sem, hsend, hrecv, load_sem):
     me = lax.axis_index("lon")
     group = lax.axis_index("groups")
@@ -118,22 +118,26 @@
         load.start()
     pl.semaphore_wait(barrier, n - 1)
 
-    def block_copy(d, slot):
-        target = lax.rem(me + d, n)
+    def block_copy(target):
         return pltpu.make_async_remote_copy(
             src_ref=lat_ref.at[:, :, pl.ds(pl.multiple_of(target * cols, cols), cols)],
-            dst_ref=recv.at[slot],
+            dst_ref=recv.at[me],
             send_sem=send_sem,
             recv_sem=recv_sem,
             device_id=(group, target),
             device_id_type=MESH,
         )
 
-    def send(d, carry):
-        block_copy(d, me).start()
+    def send(k, carry):
+        target = n - 4 - k // 4 * 4 + (me + k + 1) % 4
+
+        @pl.when(target != me)
+        def _():
+            block_copy(target).start()
+
         return carry
 
-    lax.fori_loop(1, n, send, 0)
+    lax.fori_loop(0, n, send, 0)
 
     loads[0].wait()
     p = lax.broadcasted_iota(jnp.int32, (cols, cols), 0)
@@ -170,18 +174,13 @@
 
     for q in range(per):
         edge_hot[q * edge_held : (q + 1) * edge_held] = (edge_of(edge_col_key, q, 2 * cols) == wide_hot[:edge_held]).astype(F32).astype(BF16)
-    edge_at = [edge_of(edge_row_key, q, wide) - spot[:edge_held] for q in range(per)]
+        edge_at[q * edge_held : (q + 1) * edge_held] = edge_of(edge_row_key, q, wide) - spot[:edge_held]
     for h in range(height):
         hot[h * cols : (h + 1) * cols] = (col_key[:, h : h + 1] == wide_hot).astype(F32).astype(BF16)
-    at_row = [jnp.broadcast_to(row_key[:, h : h + 1], (cols, wide)) - spot for h in range(height)]
+        at_ref[h * cols : (h + 1) * cols] = jnp.broadcast_to(row_key[:, h : h + 1], (cols, wide)) - spot
     fi = lax.broadcasted_iota(jnp.int32, (per * wide, wide), 0)
     fo = lax.broadcasted_iota(jnp.int32, (per * wide, wide), 1)
-    fold = ((fi // wide == fo // channels) & (fi % held // sub_rows == fo % channels)).astype(F32).astype(BF16)
-    for load in loads[1:]:
-        load.wait()
-    coarse_weights(kd, kc, ku, kp, wd, wc, wu, wp)
-    fine_weights(k1, k2, km, w1, wlast, wfirst, wnext, w2, wma, wmb)
-
+    fold_ref[...] = ((fi // wide == fo // channels) & (fi % held // sub_rows == fo % channels)).astype(F32).astype(BF16)
     mine.wait()
 
     blocks = pltpu.make_async_remote_copy(
@@ -196,9 +195,12 @@
 
     lead = groups * strip
     firsts, lasts = edge.at[pl.ds(0, lead)], edge.at[pl.ds(lead, lead)]
-    arrived = recv[...].reshape(n // 2, 2, held, cols)
-    source = jnp.concatenate([arrived[:, 0], arrived[:, 1]], axis=2).reshape(n // 2 * held, 2 * cols)
-    tiles = source.shape[0] // wide
+
+    def source_of():
+        arrived = recv[...].reshape(n // 2, 2, held, cols)
+        return jnp.concatenate([arrived[:, 0], arrived[:, 1]], axis=2).reshape(n // 2 * held, 2 * cols)
+
+    tiles = n // 2 * held // wide
 
     def pick(got, at, q, count):
         one = jnp.zeros((count, wide), F32)
@@ -207,21 +209,29 @@
             one = jnp.where(at == t * per_tile * sub_rows, value, one)
         return one.astype(BF16)
 
-    got = dot_nt(edge_hot[...], source)
-    picked = [pick(got, edge_at[q], q, edge_held) for q in range(per)]
-    edge[...] = jnp.dot(jnp.concatenate(picked, axis=1), fold, preferred_element_type=F32).astype(BF16)
+    got = dot_nt(edge_hot[...], source_of())
+    picked = [pick(got, edge_at[q * edge_held : (q + 1) * edge_held], q, edge_held) for q in range(per)]
+    edge[...] = jnp.dot(jnp.concatenate(picked, axis=1), fold_ref[...], preferred_element_type=F32).astype(BF16)
     for src, first_row, count, shift in (
         (lasts, cols + 4 * strip, lead, 1), (firsts, cols + 4 * strip + lead, lead, -1),
         (edge.at[pl.ds(lead, 2 * strip)], cols, 2 * strip, n // 2 + 1), (edge.at[pl.ds(0, 2 * strip)], cols + 2 * strip, 2 * strip, n // 2 - 1),
     ):
         halo(src, halo_ref.at[pl.ds(first_row, count)], shift).start()
-    for g in range(groups):
-        got = dot_nt(hot[g * per * cols : (g + 1) * per * cols], source)
-        picked = [pick(got, at_row[g * per + q], q, cols) for q in range(per)]
-        own_ref[g] = jnp.dot(jnp.concatenate(picked, axis=1), fold, preferred_element_type=F32).astype(BF16)
-        if g == 0:
-            halo(own_ref.at[0], halo_ref.at[pl.ds(0, cols)], n // 2).start()
-
+
+    @pl.when(me >= 0)
+    def _():
+        source = source_of()
+        for g in range(groups):
+            got = dot_nt(hot[g * per * cols : (g + 1) * per * cols], source)
+            picked = [pick(got, at_ref[(g * per + q) * cols : (g * per + q + 1) * cols], q, cols) for q in range(per)]
+            own_ref[g] = jnp.dot(jnp.concatenate(picked, axis=1), fold_ref[...], preferred_element_type=F32).astype(BF16)
+            if g == 0:
+                halo(own_ref.at[0], halo_ref.at[pl.ds(0, cols)], n // 2).start()
+
+    for load in loads[1:]:
+        load.wait()
+    coarse_weights(kd, kc, ku, kp, wd, wc, wu, wp)
+    fine_weights(k1, k2, km, w1, wlast, wfirst, wnext, w2, wma, wmb)
     blocks.wait_send()
     every = halo(halo_ref, halo_ref, 1)
     every.wait_send()
@@ -408,6 +418,9 @@
             pltpu.VMEM((sides, PER * channels), BF16),
             pltpu.VMEM((height * cols, 2 * cols), BF16),
             pltpu.VMEM((PER * sides, 2 * cols), BF16),
+            pltpu.VMEM((PER * sides, PER * channels), jnp.int32),
+            pltpu.VMEM((height * cols, PER * channels), jnp.int32),
+            pltpu.VMEM((PER * PER * channels, PER * channels), BF16),
             pltpu.SemaphoreType.DMA,
             pltpu.SemaphoreType.DMA,
             pltpu.SemaphoreType.DMA,

time: 22.1 us -> 21.7 us (0.982)
  Pallas kernels: 21.9 us -> 21.5 us
    pallas_call x1, Pallas kernels: 16 us -> 15.6 us  [shards(): pl.pallas_call(functools.partial(exchange_kernel, n), out_shape=(jax.Shap...]
where the time goes in v3:
time: 21.7 us; the launch traced here: 21.5 us
  Pallas kernels  21.5 us (99%)
    pallas_call x1, Pallas kernels, shards(): pl.pallas_call(functools.partial(exchange_kernel, n), out_shape=(jax.Shap...  15.6 us
    pallas_call x1, Pallas kernels, shards(): pl.pallas_call(unet_kernel, out_shape=jax.ShapeDtypeStruct((COUT, height,...  5.91 us

profile of v3, /device:TPU:0, one launch (start us, length us, event | category | flops | bytes accessed | tf_op | source)
XLA Modules:
  0.0 21.5 jit_solution(17109866533927545413)
XLA Ops:
  0.0 15.6 %exchange.1 = (bf16[4,128,128]{2,1,0:T(8,128)(2,1)S(1)}, bf16[224,128]{1,0:T(8,128)(2,1)S(1)}, bf16[512,1024]{1,0:T(8,128)(2,1)S(1)}, bf16[512,128]{1,0:T(8,128)...) custom-call(bf16[16,2,2048]{2,1,0:T(2,128)(2,1)} %lat_ref.1, ...), custom_call_target="tpu_custom_call" | custom-call | tf_op jit(solution)/shard_map/exchange/pallas_call | solution.py:409
  15.6 5.9 %unet.1 = f32[8,32,128]{2,1,0:T(8,128)} custom-call(bf16[4,128,128]{2,1,0:T(8,128)(2,1)S(1)} %get-tuple-element.18.own_ref, bf16[224,128]{1,0:T(8,128)(2,1)S(1)} %get-tuple-element.19.halo_ref, bf16[512,1024]{1,0:T(8,128)(2,1)S(1)} %get-tuple-element.20.w1, bf16[512,128]{1,0:T(8,128)(2,1)S(1)} %get-tuple-element.21.wlast, ...), custom_call_target="tpu_custom_call" | custom-call | tf_op jit(solution)/shard_map/unet/pallas_call | solution.py:436

commit v4 on v3

--- a/solution.py
+++ b/solution.py
@@ -32,6 +32,15 @@
 def clear(*arrays):
     for w in arrays:
         w[...] = jnp.zeros_like(w)
+
+
+def inner_taps(v):
+    half = v.shape[0] // 2
+    even, odd = v[:half], v[half:]
+    row = lax.broadcasted_iota(jnp.int32, even.shape, 0)
+    after = jnp.where(row == half - 1, 0.0, pltpu.roll(even, half - 1, 0))
+    before = jnp.where(row == 0, 0.0, pltpu.roll(odd, 1, 0))
+    return jnp.concatenate([even, odd, after, before], axis=1).astype(BF16)
 
 
 def fill(w, kernel, cin, first_in):
@@ -93,7 +102,7 @@
 
 
 def exchange_kernel(n, lat_ref, tab_hbm, k1_hbm, k2_hbm, kd_hbm, kc_hbm, ku_hbm, km_hbm, kp_hbm,
-                    own_ref, halo_ref, w1, wlast, wfirst, wnext, w2, wd, wc, wu, wma, wmb, wp,
+                    own_ref, halo_ref, pre_ref, w1, wlast, wfirst, wnext, w2, wd, wc, wu, wma, wmb, wp,
                     tab_ref, k1, k2, kd, kc, ku, km, kp, recv, edge, hot, edge_hot, edge_at, at_ref, fold_ref,
                     send_sem, recv_sem, own_sem, hsend, hrecv, load_sem):
     me = lax.axis_index("lon")
@@ -181,6 +190,10 @@
     fi = lax.broadcasted_iota(jnp.int32, (per * wide, wide), 0)
     fo = lax.broadcasted_iota(jnp.int32, (per * wide, wide), 1)
     fold_ref[...] = ((fi // wide == fo // channels) & (fi % held // sub_rows == fo % channels)).astype(F32).astype(BF16)
+    for load in loads[1:]:
+        load.wait()
+    coarse_weights(kd, kc, ku, kp, wd, wc, wu, wp)
+    fine_weights(k1, k2, km, w1, wlast, wfirst, wnext, w2, wma, wmb)
     mine.wait()
 
     blocks = pltpu.make_async_remote_copy(
@@ -228,17 +241,28 @@
             if g == 0:
                 halo(own_ref.at[0], halo_ref.at[pl.ds(0, cols)], n // 2).start()
 
-    for load in loads[1:]:
-        load.wait()
-    coarse_weights(kd, kc, ku, kp, wd, wc, wu, wp)
-    fine_weights(k1, k2, km, w1, wlast, wfirst, wnext, w2, wma, wmb)
+    middle = jnp.concatenate([inner_taps(own_ref[g].astype(F32)) for g in range(groups)], axis=0)
+    half, pair = cols // 2, 2 * k1.shape[3]
+    base = dot_nn(middle, w1[...])
+    above = dot_nn(middle[: (groups - 1) * half], wlast[...])
+    below = dot_nn(middle[half:], wnext[...])
+    for g in range(groups):
+        for r in range(per):
+            v = base[g * half : (g + 1) * half, r * pair : (r + 1) * pair]
+            if r == 0 and g > 0:
+                v = v + above[(g - 1) * half : g * half]
+            if r == per - 1 and g < groups - 1:
+                v = v + below[g * half : (g + 1) * half]
+            if g + r > 0:
+                v = jnp.concatenate([v[:strip], silu(v[strip : half - strip]), v[half - strip :]], axis=0)
+            pre_ref[g * per + r] = v
     blocks.wait_send()
     every = halo(halo_ref, halo_ref, 1)
     every.wait_send()
     every.wait_recv()
 
 
-def unet_kernel(own_ref, halo_ref, w1, wlast, wfirst, wnext, w2, wd, wc, wu, wma, wmb, wp, out_ref, xf, x1, x2, x3, xc, xu):
+def unet_kernel(own_ref, halo_ref, pre_ref, w1, wlast, wfirst, wnext, w2, wd, wc, wu, wma, wmb, wp, out_ref, x1, x2, x3, xc, xu):
     groups, cols, wide = own_ref.shape
     height = groups * PER
     channels = wide // PER
@@ -260,9 +284,23 @@
 
     around = halo_ref[...].astype(F32)
     corners, sides = around[cols : cols + 4 * strip], around[cols + 4 * strip :]
-    for g in range(groups):
-        xf[g] = spread(own_ref[g].astype(F32), sides[g * strip : (g + 1) * strip], sides[(groups + g) * strip : (groups + g + 1) * strip])
-    xf[groups] = spread(around[:cols], corners[:strip], corners[2 * strip : 3 * strip])
+    row = lax.broadcasted_iota(jnp.int32, (strip, wide), 0)
+    none = jnp.zeros((strip, wide), F32)
+
+    def rim(g, l, r):
+        even, odd = jnp.where(upper, r, l), pltpu.roll(jnp.where(upper, l, r), HALO, 0)
+        after = jnp.where(row == strip - 1, g[0:1], pltpu.roll(even, strip - 1, 0))
+        before = jnp.where(row == 0, g[cols - 1 : cols], pltpu.roll(odd, 1, 0))
+        ring = jnp.concatenate([even, odd, after, before], axis=1)
+        ends = jnp.concatenate([none, none, jnp.where(row == 0, even, 0.0), jnp.where(row == strip - 1, odd, 0.0)], axis=1)
+        return jnp.concatenate([ring, ends], axis=0).astype(BF16)
+
+    own = [own_ref[g].astype(F32) for g in range(groups)]
+    lefts = [sides[g * strip : (g + 1) * strip] for g in range(groups)]
+    rights = [sides[(groups + g) * strip : (groups + g + 1) * strip] for g in range(groups)]
+    rims = jnp.concatenate([rim(own[g], lefts[g], rights[g]) for g in range(groups)], axis=0)
+    top = spread(own[0], lefts[0], rights[0])
+    across = spread(around[:cols], corners[:strip], corners[2 * strip : 3 * strip])
 
     def neighbours(v):
         count = v.shape[0]
@@ -291,22 +329,37 @@
         for t in range(steps):
             body(t)
 
-    every = groups + 1
-    acc = dot_nn(xf[...].reshape(every * J, 4 * wide), w1[...]).reshape(every, J, PER * 2 * C)
-    from_last = dot_nn(xf[pl.ds(0, groups - 1)].reshape((groups - 1) * J, 4 * wide), wlast[...]).reshape(groups - 1, J, 2 * C)
-    from_next = dot_nn(xf[pl.ds(1, groups - 1)].reshape((groups - 1) * J, 4 * wide), wnext[...]).reshape(groups - 1, J, 2 * C)
-    own_top = dot_nn(xf[groups], wfirst[...])
-    anti_top = dot_nn(xf[0], wfirst[...])
-    for g in range(every):
+    R = 2 * strip
+    base = dot_nn(rims, w1[...])
+    above = dot_nn(rims[: (groups - 1) * R], wlast[...])
+    below = dot_nn(rims[R:], wnext[...])
+    own_top = dot_nn(across, wfirst[...])
+    anti_top = dot_nn(top, wfirst[...])
+    anti = dot_nn(across, w1[...])
+    for g in range(groups):
         for r in range(PER):
-            v = acc[g, :, r * 2 * C : (r + 1) * 2 * C]
-            if r == 0:
-                v = v + (anti_top if g == groups else own_top if g == 0 else from_last[g - 1])
+            e = base[g * R : (g + 1) * R, r * 2 * C : (r + 1) * 2 * C]
+            if r == 0 and g > 0:
+                e = e + above[(g - 1) * R : g * R]
             if r == PER - 1 and g < groups - 1:
-                v = v + from_next[g]
-            slot = g * PER + r + 1 + (2 if g == groups else 0)
-            if slot // 2 < x1.shape[0]:
-                x1[slot // 2, slot % 2] = neighbours(silu(v))[0]
+                e = e + below[g * R : (g + 1) * R]
+            ring, ends = e[:strip], e[strip:]
+            v = pre_ref[g * PER + r]
+            head = v[:strip] + jnp.where(row == 0, pltpu.roll(ends, 1, 0), 0.0)
+            tail = v[half - strip :] + jnp.where(row == strip - 1, pltpu.roll(ends, strip - 1, 0), 0.0)
+            inner = v[strip : half - strip]
+            if g + r > 0:
+                v = silu(jnp.concatenate([head, tail, ring], axis=0))
+                v = jnp.concatenate([v[:strip], inner, v[strip:]], axis=0)
+            else:
+                v = silu(jnp.concatenate([head, inner, tail, ring], axis=0) + own_top)
+            slot = g * PER + r + 1
+            x1[slot // 2, slot % 2] = neighbours(v)[0]
+    for r in range(PER):
+        slot = groups * PER + r + 3
+        if slot // 2 < x1.shape[0]:
+            v = anti[:, r * 2 * C : (r + 1) * 2 * C]
+            x1[slot // 2, slot % 2] = neighbours(silu(v + anti_top if r == 0 else v))[0]
     wrap(x1)
 
     def second(i0, count):
@@ -408,9 +461,10 @@
     )
     ready = pl.pallas_call(
         functools.partial(exchange_kernel, n),
-        out_shape=(jax.ShapeDtypeStruct((groups, cols, PER * channels), BF16), around) + weights,
+        out_shape=(jax.ShapeDtypeStruct((groups, cols, PER * channels), BF16), around,
+                   jax.ShapeDtypeStruct((height, cols // 2, 2 * C), F32)) + weights,
         in_specs=[pl.BlockSpec(memory_space=pltpu.HBM)] * 9,
-        out_specs=(vm,) * 13,
+        out_specs=(vm,) * 14,
         scratch_shapes=[
             pltpu.VMEM(table.shape, table.dtype),
         ] + [pltpu.VMEM(k.shape, BF16) for k in (k1, k2, kd, kc, ku, km, kp)] + [
@@ -436,10 +490,9 @@
     return pl.pallas_call(
         unet_kernel,
         out_shape=jax.ShapeDtypeStruct((COUT, height, cols), F32),
-        in_specs=[vm] * 13,
+        in_specs=[vm] * 14,
         out_specs=vm,
         scratch_shapes=[
-            pltpu.VMEM((height // PER + 1, J, 4 * PER * channels), BF16),
             pltpu.VMEM((pairs + 5, 2, J, 4 * C), BF16),
             pltpu.VMEM((pairs + 4, 2, J, 4 * C), BF16),
             pltpu.VMEM((pairs + 1, 2, J, 4 * C), BF16),

time: 21.7 us -> 21.4 us (0.986)
    pallas_call x1, Pallas kernels: 5.91 us -> 5.67 us  [shards(): pl.pallas_call(unet_kernel, out_shape=jax.ShapeDtypeStruct((COUT, height,...]
where the time goes in v4:
time: 21.4 us; the launch traced here: 21.3 us
  Pallas kernels  21.3 us (100%)
    pallas_call x1, Pallas kernels, shards(): pl.pallas_call(functools.partial(exchange_kernel, n), out_shape=(jax.Shap...  15.6 us
    pallas_call x1, Pallas kernels, shards(): pl.pallas_call(unet_kernel, out_shape=jax.ShapeDtypeStruct((COUT, height,...  5.67 us

profile of v4, /device:TPU:0, one launch (start us, length us, event | category | flops | bytes accessed | tf_op | source)
XLA Modules:
  0.0 21.3 jit_solution(17933976389948982762)
XLA Ops:
  0.0 15.6 %exchange.1 = (bf16[4,128,128]{2,1,0:T(8,128)(2,1)S(1)}, bf16[224,128]{1,0:T(8,128)(2,1)S(1)}, f32[32,64,128]{2,1,0:T(8,128)S(1)}, bf16[512,1024]{1,0:T(8,128)(2...) custom-call(bf16[16,2,2048]{2,1,0:T(2,128)(2,1)} %lat_ref.1, ...), custom_call_target="tpu_custom_call" | custom-call | tf_op jit(solution)/shard_map/exchange/pallas_call | solution.py:462
  15.6 5.7 %unet.1 = f32[8,32,128]{2,1,0:T(8,128)} custom-call(bf16[4,128,128]{2,1,0:T(8,128)(2,1)S(1)} %get-tuple-element.19.own_ref, bf16[224,128]{1,0:T(8,128)(2,1)S(1)} %get-tuple-element.20.halo_ref, f32[32,64,128]{2,1,0:T(8,128)S(1)} %get-tuple-element.21.pre_ref, bf16[512,1024]{1,0:T(8,128)(2,1)S(1)} %get-tuple-element.22.w1, ...), custom_call_target="tpu_custom_call" | custom-call | tf_op jit(solution)/shard_map/unet/pallas_call | solution.py:490

commit v5 on v4

--- a/solution.py
+++ b/solution.py
@@ -102,7 +102,7 @@
 
 
 def exchange_kernel(n, lat_ref, tab_hbm, k1_hbm, k2_hbm, kd_hbm, kc_hbm, ku_hbm, km_hbm, kp_hbm,
-                    own_ref, halo_ref, pre_ref, w1, wlast, wfirst, wnext, w2, wd, wc, wu, wma, wmb, wp,
+                    own_ref, halo_ref, pre_ref, rest_ref, w1, wlast, wfirst, wnext, w2, wd, wc, wu, wma, wmb, wp,
                     tab_ref, k1, k2, kd, kc, ku, km, kp, recv, edge, hot, edge_hot, edge_at, at_ref, fold_ref,
                     send_sem, recv_sem, own_sem, hsend, hrecv, load_sem):
     me = lax.axis_index("lon")
@@ -256,13 +256,19 @@
             if g + r > 0:
                 v = jnp.concatenate([v[:strip], silu(v[strip : half - strip]), v[half - strip :]], axis=0)
             pre_ref[g * per + r] = v
+    outputs = wp.shape[0] // 4
+    flat = [own_ref[g].astype(F32).T for g in range(groups)]
+    kept = [flat[h // per][h % per * channels : h % per * channels + outputs] for h in range(height)]
+    at = lax.broadcasted_iota(jnp.int32, (cols, cols), 0)
+    unperm = (wide_hot[:, :cols] == jnp.where(at < half, 2 * at, 2 * at - cols + 1)).astype(F32).astype(BF16)
+    rest_ref[...] = dot_nn(jnp.concatenate(kept, axis=0).astype(BF16), unperm)
     blocks.wait_send()
     every = halo(halo_ref, halo_ref, 1)
     every.wait_send()
     every.wait_recv()
 
 
-def unet_kernel(own_ref, halo_ref, pre_ref, w1, wlast, wfirst, wnext, w2, wd, wc, wu, wma, wmb, wp, out_ref, x1, x2, x3, xc, xu):
+def unet_kernel(own_ref, halo_ref, pre_ref, rest_ref, w1, wlast, wfirst, wnext, w2, wd, wc, wu, wma, wmb, wp, out_ref, x1, x2, x3, xc, xu):
     groups, cols, wide = own_ref.shape
     height = groups * PER
     channels = wide // PER
@@ -381,8 +387,8 @@
         acc = dot_nn(jnp.concatenate([taps(x2, i0, count, a, J) for a in range(3)], axis=1), wd[...])
         xc[pl.ds(slot, count)] = shifts(silu(acc), True)
 
+    own_loop(pairs // B, lambda t: down(t * B, t * B + 1, B))
     down(AB, pairs + 3, 2)
-    own_loop(pairs // B, lambda t: down(t * B, t * B + 1, B))
     xc[0] = xc[pairs + 3]
     xc[pairs + 2] = xc[1]
     xc[pairs + 1] = jnp.zeros(xc.shape[1:], BF16)
@@ -391,8 +397,8 @@
         acc = dot_nt(jnp.concatenate([xc[pl.ds(i0 + a, count)].reshape(count * J, 3 * C2) for a in range(3)], axis=1), wc[...])
         xu[pl.ds(slot, count)] = shifts(silu(acc), False)
 
+    own_loop(pairs // B, lambda t: coarse(t * B, t * B, B))
     coarse(pairs + 2, pairs + 1, 1)
-    own_loop(pairs // B, lambda t: coarse(t * B, t * B, B))
     xu[pairs] = jnp.zeros(xu.shape[1:], BF16)
 
     def up(i0, count):
@@ -411,7 +417,6 @@
     unperm = (w == jnp.where(p < half, 2 * p, 2 * p - cols + 1)).astype(F32).astype(BF16)
     unperm = jnp.concatenate([unperm, unperm], axis=0)
     wpb = wp[...].astype(BF16)
-    plain = [own_ref[g].astype(F32).T for g in range(groups)]
 
     def merge(i0, count):
         tiles = [taps(x, i0, count, a, half) for x in (x2, x3) for a in range(4)]
@@ -425,15 +430,13 @@
             u = update[:, b * half : (b + 1) * half]
             for q in range(2):
                 line = jnp.concatenate([u[2 * q * COUT : (2 * q + 1) * COUT], u[(2 * q + 1) * COUT : (2 * q + 2) * COUT]], axis=1)
-                h = 2 * (t * BM + b) + q
-                at = (h % PER) * channels
-                lines.append(line + plain[h // PER][at : at + COUT])
+                lines.append(line)
     lines = jnp.concatenate(lines, axis=0)
     high = lines.astype(BF16)
     low = (lines - high.astype(F32)).astype(BF16)
     woven = dot_nn(jnp.concatenate([high, low], axis=1), unperm)
     for h in range(height):
-        out_ref[:, h, :] = woven[h * COUT : (h + 1) * COUT]
+        out_ref[:, h, :] = woven[h * COUT : (h + 1) * COUT] + rest_ref[h * COUT : (h + 1) * COUT]
 
 
 def shards(latlon, table, k1, k2, kd, kc, ku, km, kp):
@@ -462,9 +465,10 @@
     ready = pl.pallas_call(
         functools.partial(exchange_kernel, n),
         out_shape=(jax.ShapeDtypeStruct((groups, cols, PER * channels), BF16), around,
-                   jax.ShapeDtypeStruct((height, cols // 2, 2 * C), F32)) + weights,
+                   jax.ShapeDtypeStruct((height, cols // 2, 2 * C), F32),
+                   jax.ShapeDtypeStruct((height * COUT, cols), F32)) + weights,
         in_specs=[pl.BlockSpec(memory_space=pltpu.HBM)] * 9,
-        out_specs=(vm,) * 14,
+        out_specs=(vm,) * 15,
         scratch_shapes=[
             pltpu.VMEM(table.shape, table.dtype),
         ] + [pltpu.VMEM(k.shape, BF16) for k in (k1, k2, kd, kc, ku, km, kp)] + [
@@ -490,7 +494,7 @@
     return pl.pallas_call(
         unet_kernel,
         out_shape=jax.ShapeDtypeStruct((COUT, height, cols), F32),
-        in_specs=[vm] * 14,
+        in_specs=[vm] * 15,
         out_specs=vm,
         scratch_shapes=[
             pltpu.VMEM((pairs + 5, 2, J, 4 * C), BF16),

time: 21.4 us -> 21.4 us (level)
  no operation moved by 1% of the time
where the time goes in v5:
time: 21.4 us; the launch traced here: 21.2 us
  Pallas kernels  21.2 us (99%)
    pallas_call x1, Pallas kernels, shards(): pl.pallas_call(functools.partial(exchange_kernel, n), out_shape=(jax.Shap...  15.6 us
    pallas_call x1, Pallas kernels, shards(): pl.pallas_call(unet_kernel, out_shape=jax.ShapeDtypeStruct((COUT, height,...  5.6 us

profile of v5, /device:TPU:0, one launch (start us, length us, event | category | flops | bytes accessed | tf_op | source)
XLA Modules:
  0.0 21.2 jit_solution(12962573464530667893)
XLA Ops:
  0.0 15.6 %exchange.1 = (bf16[4,128,128]{2,1,0:T(8,128)(2,1)S(1)}, bf16[224,128]{1,0:T(8,128)(2,1)S(1)}, f32[32,64,128]{2,1,0:T(8,128)S(1)}, f32[256,128]{1,0:T(8,128)S(1)...) custom-call(bf16[16,2,2048]{2,1,0:T(2,128)(2,1)} %lat_ref.1, ...), custom_call_target="tpu_custom_call" | custom-call | tf_op jit(solution)/shard_map/exchange/pallas_call | solution.py:465
  15.6 5.6 %unet.1 = f32[8,32,128]{2,1,0:T(8,128)} custom-call(bf16[4,128,128]{2,1,0:T(8,128)(2,1)S(1)} %get-tuple-element.20.own_ref, bf16[224,128]{1,0:T(8,128)(2,1)S(1)} %get-tuple-element.21.halo_ref, f32[32,64,128]{2,1,0:T(8,128)S(1)} %get-tuple-element.22.pre_ref, f32[256,128]{1,0:T(8,128)S(1)} %get-tuple-element.23.rest_ref, ...), custom_call_target="tpu_custom_call" | custom-call | tf_op jit(solution)/shard_map/unet/pallas_call | solution.py:494

commit v6 on v4

--- a/solution.py
+++ b/solution.py
@@ -381,8 +381,8 @@
         acc = dot_nn(jnp.concatenate([taps(x2, i0, count, a, J) for a in range(3)], axis=1), wd[...])
         xc[pl.ds(slot, count)] = shifts(silu(acc), True)
 
+    own_loop(pairs // B, lambda t: down(t * B, t * B + 1, B))
     down(AB, pairs + 3, 2)
-    own_loop(pairs // B, lambda t: down(t * B, t * B + 1, B))
     xc[0] = xc[pairs + 3]
     xc[pairs + 2] = xc[1]
     xc[pairs + 1] = jnp.zeros(xc.shape[1:], BF16)
@@ -391,8 +391,8 @@
         acc = dot_nt(jnp.concatenate([xc[pl.ds(i0 + a, count)].reshape(count * J, 3 * C2) for a in range(3)], axis=1), wc[...])
         xu[pl.ds(slot, count)] = shifts(silu(acc), False)
 
+    own_loop(pairs // B, lambda t: coarse(t * B, t * B, B))
     coarse(pairs + 2, pairs + 1, 1)
-    own_loop(pairs // B, lambda t: coarse(t * B, t * B, B))
     xu[pairs] = jnp.zeros(xu.shape[1:], BF16)
 
     def up(i0, count):

time: 21.4 us -> 21.4 us (level)
  no operation moved by 1% of the time
where the time goes in v6:
time: 21.4 us; the launch traced here: 21.3 us
  Pallas kernels  21.3 us (100%)
    pallas_call x1, Pallas kernels, shards(): pl.pallas_call(functools.partial(exchange_kernel, n), out_shape=(jax.Shap...  15.6 us
    pallas_call x1, Pallas kernels, shards(): pl.pallas_call(unet_kernel, out_shape=jax.ShapeDtypeStruct((COUT, height,...  5.66 us

profile of v6, /device:TPU:0, one launch (start us, length us, event | category | flops | bytes accessed | tf_op | source)
XLA Modules:
  0.0 21.3 jit_solution(14618668422346673677)
XLA Ops:
  0.0 15.6 %exchange.1 = (bf16[4,128,128]{2,1,0:T(8,128)(2,1)S(1)}, bf16[224,128]{1,0:T(8,128)(2,1)S(1)}, f32[32,64,128]{2,1,0:T(8,128)S(1)}, bf16[512,1024]{1,0:T(8,128)(2...) custom-call(bf16[16,2,2048]{2,1,0:T(2,128)(2,1)} %lat_ref.1, ...), custom_call_target="tpu_custom_call" | custom-call | tf_op jit(solution)/shard_map/exchange/pallas_call | solution.py:462
  15.6 5.7 %unet.1 = f32[8,32,128]{2,1,0:T(8,128)} custom-call(bf16[4,128,128]{2,1,0:T(8,128)(2,1)S(1)} %get-tuple-element.19.own_ref, bf16[224,128]{1,0:T(8,128)(2,1)S(1)} %get-tuple-element.20.halo_ref, f32[32,64,128]{2,1,0:T(8,128)S(1)} %get-tuple-element.21.pre_ref, bf16[512,1024]{1,0:T(8,128)(2,1)S(1)} %get-tuple-element.22.w1, ...), custom_call_target="tpu_custom_call" | custom-call | tf_op jit(solution)/shard_map/unet/pallas_call | solution.py:490
